TPU v7x, 32 devices: a whole 2x2x4 slice. The times are simulated.
32 devices in a mesh: dp: 8 (over y, x, core), tensor: 4 (over z).
Axes of the slice: x: 2, y: 2, z: 4, core: 2. Of those that a mesh axis runs over, the one named last changes fastest.
Arguments:
- hidden: bfloat16 [4096, 8192], P(('dp', 'tensor')), may hold values from -6 to 6
- norm_gain: float32 [8192], replicated, may hold values from 0.5 to 1.5
- tile_values: bfloat16 [4, 80, 128, 128], P('tensor', 'dp'), may hold values from -0.15625 to 0.15625
- tile_ids: int32 [4, 80], P('tensor', 'dp'), may hold values from 0 to 1279, as said below
- tile_counts: int32 [4, 8], P('tensor', 'dp'), may hold values from 5 to 10, as said below
- proj_grad: bfloat16 [4096, 10240], P('dp', 'tensor'), may hold values from -6 to 6
Outputs:
- projections: bfloat16 [4096, 10240], P('dp', 'tensor')
- hidden_grad: bfloat16 [4096, 8192], P(('dp', 'tensor'))
- tile_grads: float32 [4, 80, 128, 128], P('tensor', 'dp')
- gain_grad: float32 [8192], replicated
Inputs may be any that keep to these rules, and one draw needn't show every extreme that they name: `tile_ids`: within each tensor index the 80 block numbers are distinct; a slot's number holds whether or not the slot is live. `tile_counts`: for every tensor index some owner has all 10 slots live.
All inputs are finite; a program needn't handle non-finite values.
Results may differ from a plain program's by a relative error of at most 0.013.
Values may be sent and summed in bfloat16 or wider, within the bound.
A program may use at most 192 MiB of HBM per device.

v0:
```python
import math
import jax
import jax.numpy as jnp
from jax import lax
from jax.sharding import PartitionSpec as P

EPSILON = 1e-05


def normalize(source, norm_gain):
    source_f = source.astype(jnp.float32)
    inverse = lax.rsqrt(jnp.mean(source_f * source_f, axis=-1, keepdims=True) + EPSILON)
    return (source_f, inverse, (source_f * inverse * norm_gain).astype(jnp.bfloat16))


def selector(block_names, total_count):
    return (block_names[:, None] == jnp.arange(total_count, dtype=jnp.int32)[None, :]).astype(
        jnp.bfloat16
    )


def pick_tiles(blocks, block_names, total_count):
    chooser = selector(block_names, total_count)
    return jnp.einsum("nri,sr->nsi", blocks, chooser, preferred_element_type=jnp.float32).astype(
        jnp.bfloat16
    )


def place_tiles(values, block_names, total_count):
    chooser = selector(block_names, total_count)
    upper_half = values.astype(jnp.bfloat16)
    lower_half = (values - upper_half.astype(jnp.float32)).astype(jnp.bfloat16)
    placed = jnp.einsum("nsi,sr->nri", upper_half, chooser, preferred_element_type=jnp.float32)
    return placed + jnp.einsum(
        "nsi,sr->nri", lower_half, chooser, preferred_element_type=jnp.float32
    )


def over_groups(handler, running, tile_block, tile_names, anchor, slot_count):
    group_total = tile_names.shape[0] // slot_count

    def loop_step(group_idx, state):
        offset = group_idx * slot_count
        block_vals = lax.dynamic_slice_in_dim(tile_block, offset, slot_count, 0)
        block_names = lax.dynamic_slice_in_dim(tile_names, offset, slot_count, 0)
        return handler(state, block_vals, block_names, anchor + offset)

    return lax.fori_loop(0, group_total, loop_step, running)


def body(hidden, norm_gain, tile_values, tile_ids, tile_counts, proj_grad):
    model_width = hidden.shape[1]
    tile_size = tile_values.shape[-1]
    slot_count = tile_values.shape[1]
    seq_rows = proj_grad.shape[0]
    col_tiles = proj_grad.shape[1] // tile_size
    row_tiles = model_width // tile_size
    live_mask = (jnp.arange(slot_count) < tile_counts[0, 0]).astype(jnp.bfloat16)
    masked = tile_values[0] * live_mask[:, None, None]
    own_names = tile_ids[0]
    hidden_f, inverse, normed = normalize(hidden, norm_gain)
    gathered = lax.all_gather(normed, "tensor", axis=0, tiled=True)
    x_blocks = gathered.reshape(seq_rows, row_tiles, tile_size)
    g_blocks = proj_grad.reshape(seq_rows, col_tiles, tile_size)

    def forward_group(running, block_vals, block_names, offset):
        picked = pick_tiles(x_blocks, block_names // col_tiles, row_tiles)
        parts = jnp.einsum("nsi,sij->nsj", picked, block_vals, preferred_element_type=jnp.float32)
        return running + place_tiles(parts, block_names % col_tiles, col_tiles)

    start_out = jnp.zeros((seq_rows, col_tiles, tile_size), jnp.float32)
    all_vals, all_names = (
        lax.all_gather(masked, "dp", axis=0, tiled=True),
        lax.all_gather(own_names, "dp", axis=0, tiled=True),
    )
    outputs = over_groups(forward_group, start_out, all_vals, all_names, 0, slot_count)
    projections = outputs.reshape(seq_rows, col_tiles * tile_size).astype(jnp.bfloat16)
    slot_total_all = all_names.shape[0]

    def row_grad_of(g_part):

        def backward_group(local_grad, block_vals, block_names, offset):
            picked_g = pick_tiles(g_part, block_names % col_tiles, col_tiles)
            backward = jnp.einsum(
                "nsj,sij->nsi", picked_g, block_vals, preferred_element_type=jnp.float32
            )
            return local_grad + place_tiles(backward, block_names // col_tiles, row_tiles)

        start_grad = jnp.zeros((g_part.shape[0], row_tiles, tile_size), jnp.float32)
        local_grad = over_groups(backward_group, start_grad, all_vals, all_names, 0, slot_count)
        return local_grad.reshape(g_part.shape[0], model_width).astype(jnp.bfloat16)

    def tile_grad_of(weight_grad, x_part, g_part):

        def tile_group(tile_acc, block_vals, block_names, offset):
            picked_x = pick_tiles(x_part, block_names // col_tiles, row_tiles)
            picked_g = pick_tiles(g_part, block_names % col_tiles, col_tiles)
            tile_part = jnp.einsum(
                "nsi,nsj->sij", picked_x, picked_g, preferred_element_type=jnp.float32
            )
            current = lax.dynamic_slice_in_dim(tile_acc, offset, tile_part.shape[0], 0)
            return lax.dynamic_update_slice_in_dim(tile_acc, current + tile_part, offset, 0)

        return over_groups(tile_group, weight_grad, all_vals, all_names, 0, slot_count)

    block_rows = math.gcd(seq_rows, 256)
    start_tiles = jnp.zeros((slot_total_all, tile_size, tile_size), jnp.float32)

    def row_block(block_idx, state):
        row_grad, weight_grad = state
        begin = block_idx * block_rows
        x_part = lax.dynamic_slice_in_dim(x_blocks, begin, block_rows, 0)
        g_part = lax.dynamic_slice_in_dim(g_blocks, begin, block_rows, 0)
        rounded = row_grad_of(g_part)
        row_grad = lax.dynamic_update_slice_in_dim(row_grad, rounded, begin, 0)
        weight_grad = tile_grad_of(weight_grad, x_part, g_part)
        return (row_grad, weight_grad)

    initial_back = (jnp.zeros((seq_rows, model_width), jnp.bfloat16), start_tiles)
    row_grad, weight_grad = lax.fori_loop(0, seq_rows // block_rows, row_block, initial_back)
    row_sum = lax.psum_scatter(row_grad, "tensor", scatter_dimension=0, tiled=True).astype(
        jnp.float32
    )
    tile_sum = lax.psum_scatter(
        weight_grad.astype(jnp.bfloat16), "dp", scatter_dimension=0, tiled=True
    ).astype(jnp.float32)
    tile_grads = (tile_sum * live_mask.astype(jnp.float32)[:, None, None])[None]
    unit = hidden_f * inverse
    gain_part = jnp.sum(row_sum * unit, axis=0)
    gain_grad = lax.psum(gain_part, ("dp", "tensor"))
    scaled = row_sum * norm_gain
    hidden_grad = (
        inverse * (scaled - unit * jnp.mean(scaled * unit, axis=-1, keepdims=True))
    ).astype(jnp.bfloat16)
    return (projections, hidden_grad, tile_grads, gain_grad)


def solution(mesh):
    in_specs = (
        P(("dp", "tensor"), None),
        P(),
        P("tensor", "dp", None, None),
        P("tensor", "dp"),
        P("tensor", "dp"),
        P("dp", "tensor"),
    )
    out_specs = (P("dp", "tensor"), P(("dp", "tensor"), None), P("tensor", "dp", None, None), P())
    return jax.shard_map(body, mesh=mesh, in_specs=in_specs, out_specs=out_specs, check_vma=False)
```

profile of v0, /device:TPU:0, one launch (start us, length us, event | category | flops | bytes accessed | tf_op | source)
XLA Modules:
  0.0 951.3 jit_solution(16404277503629230293)
XLA Ops:
  29.8 135.6 %all-gather.6.cloned.1.call-done = bf16[512,8192]{1,0:T(8,128)(2,1)} async-done(((bf16[128,8192]{1,0:T(8,128)(2,1)}), bf16[512,8192]{1,0:T(8,128)(2,1)}) %all-gather.6.cloned.1.call-update) | async-done | bytes 8388624 | tf_op jit(solution)/shard_map/all_gather | solution.py:62
  174.7 21.4 %all-gather.4.cloned.1.call-done = bf16[80,128,128]{2,1,0:T(8,128)(2,1)} async-done(((bf16[10,128,128]{2,1,0:T(8,128)(2,1)}), bf16[80,128,128]{2,1,0:T(8,128)(2,1)}) %all-gather.4.cloned.1.call-update) | async-done | bytes 2621456 | tf_op jit(solution)/shard_map/all_gather | solution.py:73
  203.4 463.0 %while.101 = (s32[]{:T(128)}, bf16[512,8192]{1,0:T(8,128)(2,1)}, f32[80,128,128]{2,1,0:T(8,128)}, bf16[512,20,128]{0,2,1:T(8,128)(2,1)}, s32[80]{0:T(128)S(1)}, ...) while((s32[]{:T(128)}, bf16[512,8192]{1,0:T(8,128)(2,1)}, ...), condition=%wide.region_8.9_spmd, body=%wide.region_3.8_spmd.sunk | while | flops 330664448 | bytes 85787744 | solution.py:120
  205.9 162.2 %while.103 = (s32[]{:T(128)}, f32[256,64,128]{2,1,0:T(8,128)}, s32[80]{0:T(128)S(1)}, bf16[80,128,128]{2,1,0:T(8,128)(2,1)}, bf16[256,20,128]{2,1,0:T(8,128)(2,1...) while((s32[]{:T(128)}, f32[256,64,128]{2,1,0:T(8,128)}, s32[80]{0:T(128)S(1)}, ...), condition=%wide.region_5.5_spmd.clone, body=%wide.region_4.4_spmd.clone.sunk | while | flops 188810816 | bytes 41746828 | solution.py:48
  234.3 10.4 %bitcast_add_fusion.5 = f32[256,64,128]{2,1,0:T(8,128)} fusion(f32[256,64,128]{2,1,0:T(8,128)} %get-tuple-element.990, f32[64,256,128]{2,0,1:T(8,128)} %fusion.97, pred[]{:T(512)S(6)} %compare.7, bf16[256,10,128]{2,1,0:T(8,128)(2,1)S(1)} %copy.73, s32[10]{0:T(128)S(1)} %get-tuple-element.971), kind=kOutput, calls=%fused_computation.16.clone.1 | convolution fusion | flops 48235136 | bytes 25821224 | tf_op jit(solution)/shard_map/while/body/eval_jaxpr/while/body/eval_jaxpr/nsi,sr->nri/dot_general | solution.py:34
  254.8 10.4 %bitcast_add_fusion.5 = f32[256,64,128]{2,1,0:T(8,128)} fusion(f32[256,64,128]{2,1,0:T(8,128)} %get-tuple-element.990, f32[64,256,128]{2,0,1:T(8,128)} %fusion.97, pred[]{:T(512)S(6)} %compare.7, bf16[256,10,128]{2,1,0:T(8,128)(2,1)S(1)} %copy.73, s32[10]{0:T(128)S(1)} %get-tuple-element.971), kind=kOutput, calls=%fused_computation.16.clone.1 | convolution fusion | flops 48235136 | bytes 25821224 | tf_op jit(solution)/shard_map/while/body/eval_jaxpr/while/body/eval_jaxpr/nsi,sr->nri/dot_general | solution.py:34
  275.4 10.4 %bitcast_add_fusion.5 = f32[256,64,128]{2,1,0:T(8,128)} fusion(f32[256,64,128]{2,1,0:T(8,128)} %get-tuple-element.990, f32[64,256,128]{2,0,1:T(8,128)} %fusion.97, pred[]{:T(512)S(6)} %compare.7, bf16[256,10,128]{2,1,0:T(8,128)(2,1)S(1)} %copy.73, s32[10]{0:T(128)S(1)} %get-tuple-element.971), kind=kOutput, calls=%fused_computation.16.clone.1 | convolution fusion | flops 48235136 | bytes 25821224 | tf_op jit(solution)/shard_map/while/body/eval_jaxpr/while/body/eval_jaxpr/nsi,sr->nri/dot_general | solution.py:34
  296.0 10.4 %bitcast_add_fusion.5 = f32[256,64,128]{2,1,0:T(8,128)} fusion(f32[256,64,128]{2,1,0:T(8,128)} %get-tuple-element.990, f32[64,256,128]{2,0,1:T(8,128)} %fusion.97, pred[]{:T(512)S(6)} %compare.7, bf16[256,10,128]{2,1,0:T(8,128)(2,1)S(1)} %copy.73, s32[10]{0:T(128)S(1)} %get-tuple-element.971), kind=kOutput, calls=%fused_computation.16.clone.1 | convolution fusion | flops 48235136 | bytes 25821224 | tf_op jit(solution)/shard_map/while/body/eval_jaxpr/while/body/eval_jaxpr/nsi,sr->nri/dot_general | solution.py:34
  316.5 10.4 %bitcast_add_fusion.5 = f32[256,64,128]{2,1,0:T(8,128)} fusion(f32[256,64,128]{2,1,0:T(8,128)} %get-tuple-element.990, f32[64,256,128]{2,0,1:T(8,128)} %fusion.97, pred[]{:T(512)S(6)} %compare.7, bf16[256,10,128]{2,1,0:T(8,128)(2,1)S(1)} %copy.73, s32[10]{0:T(128)S(1)} %get-tuple-element.971), kind=kOutput, calls=%fused_computation.16.clone.1 | convolution fusion | flops 48235136 | bytes 25821224 | tf_op jit(solution)/shard_map/while/body/eval_jaxpr/while/body/eval_jaxpr/nsi,sr->nri/dot_general | solution.py:34
  337.1 10.4 %bitcast_add_fusion.5 = f32[256,64,128]{2,1,0:T(8,128)} fusion(f32[256,64,128]{2,1,0:T(8,128)} %get-tuple-element.990, f32[64,256,128]{2,0,1:T(8,128)} %fusion.97, pred[]{:T(512)S(6)} %compare.7, bf16[256,10,128]{2,1,0:T(8,128)(2,1)S(1)} %copy.73, s32[10]{0:T(128)S(1)} %get-tuple-element.971), kind=kOutput, calls=%fused_computation.16.clone.1 | convolution fusion | flops 48235136 | bytes 25821224 | tf_op jit(solution)/shard_map/while/body/eval_jaxpr/while/body/eval_jaxpr/nsi,sr->nri/dot_general | solution.py:34
  357.7 10.4 %bitcast_add_fusion.5 = f32[256,64,128]{2,1,0:T(8,128)} fusion(f32[256,64,128]{2,1,0:T(8,128)} %get-tuple-element.990, f32[64,256,128]{2,0,1:T(8,128)} %fusion.97, pred[]{:T(512)S(6)} %compare.7, bf16[256,10,128]{2,1,0:T(8,128)(2,1)S(1)} %copy.73, s32[10]{0:T(128)S(1)} %get-tuple-element.971), kind=kOutput, calls=%fused_computation.16.clone.1 | convolution fusion | flops 48235136 | bytes 25821224 | tf_op jit(solution)/shard_map/while/body/eval_jaxpr/while/body/eval_jaxpr/nsi,sr->nri/dot_general | solution.py:34
  387.7 47.1 %while.104 = (s32[]{:T(128)}, f32[80,128,128]{2,1,0:T(8,128)}, s32[80]{0:T(128)S(1)}, bf16[256,64,128]{2,1,0:T(8,128)(2,1)}, bf16[256,20,128]{2,1,0:T(8,128)(2,1...) while((s32[]{:T(128)}, f32[80,128,128]{2,1,0:T(8,128)}, s32[80]{0:T(128)S(1)}, ...), condition=%wide.region_7.7_spmd, body=%wide.region_6.6_spmd.sunk | while | flops 139756480 | bytes 9437531 | solution.py:48
  437.4 162.2 %while.103 = (s32[]{:T(128)}, f32[256,64,128]{2,1,0:T(8,128)}, s32[80]{0:T(128)S(1)}, bf16[80,128,128]{2,1,0:T(8,128)(2,1)}, bf16[256,20,128]{2,1,0:T(8,128)(2,1...) while((s32[]{:T(128)}, f32[256,64,128]{2,1,0:T(8,128)}, s32[80]{0:T(128)S(1)}, ...), condition=%wide.region_5.5_spmd.clone, body=%wide.region_4.4_spmd.clone.sunk | while | flops 188810816 | bytes 41746828 | solution.py:48
  465.7 10.4 %bitcast_add_fusion.5 = f32[256,64,128]{2,1,0:T(8,128)} fusion(f32[256,64,128]{2,1,0:T(8,128)} %get-tuple-element.990, f32[64,256,128]{2,0,1:T(8,128)} %fusion.97, pred[]{:T(512)S(6)} %compare.7, bf16[256,10,128]{2,1,0:T(8,128)(2,1)S(1)} %copy.73, s32[10]{0:T(128)S(1)} %get-tuple-element.971), kind=kOutput, calls=%fused_computation.16.clone.1 | convolution fusion | flops 48235136 | bytes 25821224 | tf_op jit(solution)/shard_map/while/body/eval_jaxpr/while/body/eval_jaxpr/nsi,sr->nri/dot_general | solution.py:34
  486.3 10.4 %bitcast_add_fusion.5 = f32[256,64,128]{2,1,0:T(8,128)} fusion(f32[256,64,128]{2,1,0:T(8,128)} %get-tuple-element.990, f32[64,256,128]{2,0,1:T(8,128)} %fusion.97, pred[]{:T(512)S(6)} %compare.7, bf16[256,10,128]{2,1,0:T(8,128)(2,1)S(1)} %copy.73, s32[10]{0:T(128)S(1)} %get-tuple-element.971), kind=kOutput, calls=%fused_computation.16.clone.1 | convolution fusion | flops 48235136 | bytes 25821224 | tf_op jit(solution)/shard_map/while/body/eval_jaxpr/while/body/eval_jaxpr/nsi,sr->nri/dot_general | solution.py:34
  506.9 10.4 %bitcast_add_fusion.5 = f32[256,64,128]{2,1,0:T(8,128)} fusion(f32[256,64,128]{2,1,0:T(8,128)} %get-tuple-element.990, f32[64,256,128]{2,0,1:T(8,128)} %fusion.97, pred[]{:T(512)S(6)} %compare.7, bf16[256,10,128]{2,1,0:T(8,128)(2,1)S(1)} %copy.73, s32[10]{0:T(128)S(1)} %get-tuple-element.971), kind=kOutput, calls=%fused_computation.16.clone.1 | convolution fusion | flops 48235136 | bytes 25821224 | tf_op jit(solution)/shard_map/while/body/eval_jaxpr/while/body/eval_jaxpr/nsi,sr->nri/dot_general | solution.py:34
  527.4 10.4 %bitcast_add_fusion.5 = f32[256,64,128]{2,1,0:T(8,128)} fusion(f32[256,64,128]{2,1,0:T(8,128)} %get-tuple-element.990, f32[64,256,128]{2,0,1:T(8,128)} %fusion.97, pred[]{:T(512)S(6)} %compare.7, bf16[256,10,128]{2,1,0:T(8,128)(2,1)S(1)} %copy.73, s32[10]{0:T(128)S(1)} %get-tuple-element.971), kind=kOutput, calls=%fused_computation.16.clone.1 | convolution fusion | flops 48235136 | bytes 25821224 | tf_op jit(solution)/shard_map/while/body/eval_jaxpr/while/body/eval_jaxpr/nsi,sr->nri/dot_general | solution.py:34
  548.0 10.4 %bitcast_add_fusion.5 = f32[256,64,128]{2,1,0:T(8,128)} fusion(f32[256,64,128]{2,1,0:T(8,128)} %get-tuple-element.990, f32[64,256,128]{2,0,1:T(8,128)} %fusion.97, pred[]{:T(512)S(6)} %compare.7, bf16[256,10,128]{2,1,0:T(8,128)(2,1)S(1)} %copy.73, s32[10]{0:T(128)S(1)} %get-tuple-element.971), kind=kOutput, calls=%fused_computation.16.clone.1 | convolution fusion | flops 48235136 | bytes 25821224 | tf_op jit(solution)/shard_map/while/body/eval_jaxpr/while/body/eval_jaxpr/nsi,sr->nri/dot_general | solution.py:34
  568.6 10.4 %bitcast_add_fusion.5 = f32[256,64,128]{2,1,0:T(8,128)} fusion(f32[256,64,128]{2,1,0:T(8,128)} %get-tuple-element.990, f32[64,256,128]{2,0,1:T(8,128)} %fusion.97, pred[]{:T(512)S(6)} %compare.7, bf16[256,10,128]{2,1,0:T(8,128)(2,1)S(1)} %copy.73, s32[10]{0:T(128)S(1)} %get-tuple-element.971), kind=kOutput, calls=%fused_computation.16.clone.1 | convolution fusion | flops 48235136 | bytes 25821224 | tf_op jit(solution)/shard_map/while/body/eval_jaxpr/while/body/eval_jaxpr/nsi,sr->nri/dot_general | solution.py:34
  589.1 10.4 %bitcast_add_fusion.5 = f32[256,64,128]{2,1,0:T(8,128)} fusion(f32[256,64,128]{2,1,0:T(8,128)} %get-tuple-element.990, f32[64,256,128]{2,0,1:T(8,128)} %fusion.97, pred[]{:T(512)S(6)} %compare.7, bf16[256,10,128]{2,1,0:T(8,128)(2,1)S(1)} %copy.73, s32[10]{0:T(128)S(1)} %get-tuple-element.971), kind=kOutput, calls=%fused_computation.16.clone.1 | convolution fusion | flops 48235136 | bytes 25821224 | tf_op jit(solution)/shard_map/while/body/eval_jaxpr/while/body/eval_jaxpr/nsi,sr->nri/dot_general | solution.py:34
  604.0 10.1 %bitcast_dynamic-update-slice_fusion.3 = bf16[512,8192]{1,0:T(8,128)(2,1)} fusion(bf16[512,8192]{1,0:T(8,128)(2,1)} %get-tuple-element.1081, s32[]{:T(128)S(6)} %select_n.148, bf16[32,8,64,128]{3,2,1,0:T(8,128)(2,1)S(1)} %bitcast.116), kind=kLoop, calls=%fused_computation.34.clone.1 | loop fusion | bytes 8388612 | tf_op jit(solution)/shard_map/while/body/eval_jaxpr/dynamic_update_slice | solution.py:115
  619.2 47.1 %while.104 = (s32[]{:T(128)}, f32[80,128,128]{2,1,0:T(8,128)}, s32[80]{0:T(128)S(1)}, bf16[256,64,128]{2,1,0:T(8,128)(2,1)}, bf16[256,20,128]{2,1,0:T(8,128)(2,1...) while((s32[]{:T(128)}, f32[80,128,128]{2,1,0:T(8,128)}, s32[80]{0:T(128)S(1)}, ...), condition=%wide.region_7.7_spmd, body=%wide.region_6.6_spmd.sunk | while | flops 139756480 | bytes 9437531 | solution.py:48
  671.5 213.0 %while.102 = (s32[]{:T(128)}, f32[512,20,128]{2,1,0:T(8,128)}, s32[80]{0:T(128)S(1)}, bf16[80,128,128]{2,1,0:T(8,128)(2,1)}, bf16[512,64,128]{2,1,0:T(8,128)(2,1...) while((s32[]{:T(128)}, f32[512,20,128]{2,1,0:T(8,128)}, s32[80]{0:T(128)S(1)}, ...), condition=%wide.region_2.3_spmd.clone, body=%wide.region_1.2_spmd.clone.sunk | while | flops 311297152 | bytes 42795404 | solution.py:48
  899.9 40.2 %psum.7 = f32[8192]{0:T(1024)} all-reduce(f32[8192]{0:T(1024)S(1)} %get-tuple-element.743), channel_id=1, replica_groups=mesh['dp'=8,'tensor'=4] {'dp','tensor'}, use_global_device_ids=true, to_apply=%region_13.14 | all-reduce | flops 8192 | bytes 65536 | tf_op jit(solution)/shard_map/psum | solution.py:130
  (273 shorter events, 582.4 us)
Async XLA Ops:
  7.2 6.4 copy-start
  7.2 158.2 %all-gather.6.cloned.1.call-start = ((), (), s32[]{:S(2)}) async-start(), calls=%async_computation.3 | async-start | bytes 10485760 | tf_op jit(solution)/shard_map/all_gather | solution.py:62
  9.3 9.5 %copy-start.2 = (f32[128]{0:T(128)}, f32[128]{0:T(128)S(1)}, u32[]{:S(2)}) copy-start(f32[128]{0:T(128)S(1)} %add_rsqrt_fusion) | copy-start | bytes 1540
  12.8 6.0 copy-start.5
  12.9 7.4 copy-start.4
  12.9 183.3 %all-gather.4.cloned.1.call-start = ((), (), s32[]{:S(2)}) async-start(), calls=%async_computation.2 | async-start | bytes 2949120 | tf_op jit(solution)/shard_map/all_gather | solution.py:73
  14.4 879.8 %reduce-scatter.5.cloned.1.call-start = ((), (), s32[]{:S(2)}) async-start(), calls=%async_computation.5 | async-start | bytes 2949120 | tf_op jit(solution)/shard_map/reduce_scatter | solution.py:124
  670.9 225.2 %reduce-scatter.3.cloned.1.call-start = ((), (), s32[]{:S(2)}) async-start(), calls=%async_computation.4 | async-start | bytes 10485760 | tf_op jit(solution)/shard_map/reduce_scatter | solution.py:121
  889.8 6.3 copy-start.1
  889.8 6.3 copy-start.3
Sparse Core Ops, SparseCore 0:
  13.0 152.3 all-gather.5
  167.8 28.3 all-gather.3
  671.1 43.6 reduce-scatter.4
  717.0 144.4 reduce-scatter.2
where the time goes:
time: 955 us; the launch traced here: 951 us
  matrix products  535 us (56%)
  local copies, waits for them, and re-layouts  159 us (17%)
  waiting for transfers between devices  158 us (17%)
  blocking collectives  49.7 us (5%)
  other arithmetic  33.7 us (4%)
  between operations  15.2 us (2%)
    dot_general x24, matrix products, place_tiles(): jnp.einsum('nsi,sr->nri', lower_half, chooser, preferred_element_type=jnp...  232 us
    all_gather x1, waiting for transfers between devices, body(): gathered = lax.all_gather(normed, 'tensor', axis=0, tiled=True)  136 us
    dot_general x24, matrix products, place_tiles(): jnp.einsum('nsi,sr->nri', upper_half, chooser, preferred_element_type=jnp...  115 us
    dot_general x56, matrix products, pick_tiles(): jnp.einsum('nri,sr->nsi', blocks, chooser, preferred_element_type=jnp.flo...  99.9 us
    convert_element_type x24, local copies, waits for them, and re-layouts, place_tiles(): upper_half = values.astype(jnp.bfloat16)  53.1 us
    psum x1, blocking collectives, body(): gain_grad = lax.psum(gain_part, ('dp', 'tensor'))  40.2 us
    convert_element_type x24, local copies, waits for them, and re-layouts, place_tiles(): lower_half = (values - upper_half.astype(jnp.float32)).astype(jnp.bfloat16)  39.5 us
    dot_general x16, matrix products, tile_group(): jnp.einsum('nsi,nsj->sij', picked_x, picked_g, preferred_element_type=jnp...  38.1 us
  transfers between devices with their start and end apart: 4, of which 2 were waited for; matrix products, arithmetic and copies ran while one was open for 25% of the time, Pallas kernels for 0%

commit v1 on v0

--- a/solution.py
+++ b/solution.py
@@ -127,7 +127,7 @@
     tile_grads = (tile_sum * live_mask.astype(jnp.float32)[:, None, None])[None]
     unit = hidden_f * inverse
     gain_part = jnp.sum(row_sum * unit, axis=0)
-    gain_grad = lax.psum(gain_part, ("dp", "tensor"))
+    gain_grad = jnp.sum(lax.all_gather(gain_part, ("dp", "tensor")), 0)
     scaled = row_sum * norm_gain
     hidden_grad = (
         inverse * (scaled - unit * jnp.mean(scaled * unit, axis=-1, keepdims=True))

time: 955 us -> 952 us (level)
  waiting for transfers between devices: 158 us -> 209 us
  blocking collectives: 49.7 us -> 9.46 us
  matrix products: 535 us -> 525 us
    all_gather x0 -> x1, waiting for transfers between devices: none -> 49.9 us  [body(): gain_grad = jnp.sum(lax.all_gather(gain_part, ('dp', 'tensor')), 0)]
    psum x1 -> x0, blocking collectives: 40.2 us -> none  [body(): gain_grad = lax.psum(gain_part, ('dp', 'tensor'))]
    dot_general x24, matrix products: 115 us -> 102 us  [place_tiles(): jnp.einsum('nsi,sr->nri', upper_half, chooser, preferred_element_type=jnp...]
  transfers between devices with their start and end apart: 4 -> 5, of which waited for: 2 -> 3; matrix products, arithmetic and copies ran while one was open for 25% -> 24% of each run, Pallas kernels for 0% -> 0%
where the time goes in v1:
time: 952 us; the launch traced here: 948 us
  matrix products  525 us (55%)
  waiting for transfers between devices  209 us (22%)
  local copies, waits for them, and re-layouts  155 us (16%)
  other arithmetic  33.8 us (4%)
  between operations  15.2 us (2%)
    dot_general x24, matrix products, place_tiles(): jnp.einsum('nsi,sr->nri', lower_half, chooser, preferred_element_type=jnp...  226 us
    all_gather x1, waiting for transfers between devices, body(): gathered = lax.all_gather(normed, 'tensor', axis=0, tiled=True)  137 us
    dot_general x24, matrix products, place_tiles(): jnp.einsum('nsi,sr->nri', upper_half, chooser, preferred_element_type=jnp...  102 us
    dot_general x56, matrix products, pick_tiles(): jnp.einsum('nri,sr->nsi', blocks, chooser, preferred_element_type=jnp.flo...  100 us
    convert_element_type x24, local copies, waits for them, and re-layouts, place_tiles(): upper_half = values.astype(jnp.bfloat16)  55.8 us
    all_gather x1, waiting for transfers between devices, body(): gain_grad = jnp.sum(lax.all_gather(gain_part, ('dp', 'tensor')), 0)  49.9 us
    dot_general x16, matrix products, tile_group(): jnp.einsum('nsi,nsj->sij', picked_x, picked_g, preferred_element_type=jnp...  38.2 us
    dot_general x16, matrix products, backward_group(): jnp.einsum('nsj,sij->nsi', picked_g, block_vals, preferred_element_type=j...  34.7 us
  transfers between devices with their start and end apart: 5, of which 3 were waited for; matrix products, arithmetic and copies ran while one was open for 24% of the time, Pallas kernels for 0%

profile of v1, /device:TPU:0, one launch (start us, length us, event | category | flops | bytes accessed | tf_op | source)
XLA Modules:
  0.0 948.2 jit_solution(10364356110724506348)
XLA Ops:
  28.6 137.4 %all-gather.8.cloned.1.call-done = bf16[512,8192]{1,0:T(8,128)(2,1)} async-done(((bf16[128,8192]{1,0:T(8,128)(2,1)}), bf16[512,8192]{1,0:T(8,128)(2,1)}) %all-gather.8.cloned.1.call-update) | async-done | bytes 8388624 | tf_op jit(solution)/shard_map/all_gather | solution.py:62
  175.4 21.4 %all-gather.6.cloned.1.call-done = bf16[80,128,128]{2,1,0:T(8,128)(2,1)} async-done(((bf16[10,128,128]{2,1,0:T(8,128)(2,1)}), bf16[80,128,128]{2,1,0:T(8,128)(2,1)}) %all-gather.6.cloned.1.call-update) | async-done | bytes 2621456 | tf_op jit(solution)/shard_map/all_gather | solution.py:73
  204.0 462.5 %while.101 = (s32[]{:T(128)}, bf16[512,8192]{1,0:T(8,128)(2,1)}, f32[80,128,128]{2,1,0:T(8,128)}, bf16[512,20,128]{0,2,1:T(8,128)(2,1)}, s32[80]{0:T(128)S(1)}, ...) while((s32[]{:T(128)}, bf16[512,8192]{1,0:T(8,128)(2,1)}, ...), condition=%wide.region_8.9_spmd, body=%wide.region_3.8_spmd.sunk | while | flops 330664448 | bytes 85787744 | solution.py:120
  206.6 161.9 %while.103 = (s32[]{:T(128)}, f32[256,64,128]{2,1,0:T(8,128)}, s32[80]{0:T(128)S(1)}, bf16[80,128,128]{2,1,0:T(8,128)(2,1)}, bf16[256,20,128]{2,1,0:T(8,128)(2,1...) while((s32[]{:T(128)}, f32[256,64,128]{2,1,0:T(8,128)}, s32[80]{0:T(128)S(1)}, ...), condition=%wide.region_5.5_spmd.clone, body=%wide.region_4.4_spmd.clone.sunk | while | flops 188810816 | bytes 41746828 | solution.py:48
  234.9 10.4 %bitcast_add_fusion.5 = f32[256,64,128]{2,1,0:T(8,128)} fusion(f32[256,64,128]{2,1,0:T(8,128)} %get-tuple-element.1006, f32[64,256,128]{2,0,1:T(8,128)} %fusion.97, pred[]{:T(512)S(6)} %compare.7, bf16[256,10,128]{2,1,0:T(8,128)(2,1)S(1)} %copy.86, s32[10]{0:T(128)S(1)} %get-tuple-element.987), kind=kOutput, calls=%fused_computation.16.clone.1 | convolution fusion | flops 48235136 | bytes 25821224 | tf_op jit(solution)/shard_map/while/body/eval_jaxpr/while/body/eval_jaxpr/nsi,sr->nri/dot_general | solution.py:34
  255.4 10.4 %bitcast_add_fusion.5 = f32[256,64,128]{2,1,0:T(8,128)} fusion(f32[256,64,128]{2,1,0:T(8,128)} %get-tuple-element.1006, f32[64,256,128]{2,0,1:T(8,128)} %fusion.97, pred[]{:T(512)S(6)} %compare.7, bf16[256,10,128]{2,1,0:T(8,128)(2,1)S(1)} %copy.86, s32[10]{0:T(128)S(1)} %get-tuple-element.987), kind=kOutput, calls=%fused_computation.16.clone.1 | convolution fusion | flops 48235136 | bytes 25821224 | tf_op jit(solution)/shard_map/while/body/eval_jaxpr/while/body/eval_jaxpr/nsi,sr->nri/dot_general | solution.py:34
  276.0 10.4 %bitcast_add_fusion.5 = f32[256,64,128]{2,1,0:T(8,128)} fusion(f32[256,64,128]{2,1,0:T(8,128)} %get-tuple-element.1006, f32[64,256,128]{2,0,1:T(8,128)} %fusion.97, pred[]{:T(512)S(6)} %compare.7, bf16[256,10,128]{2,1,0:T(8,128)(2,1)S(1)} %copy.86, s32[10]{0:T(128)S(1)} %get-tuple-element.987), kind=kOutput, calls=%fused_computation.16.clone.1 | convolution fusion | flops 48235136 | bytes 25821224 | tf_op jit(solution)/shard_map/while/body/eval_jaxpr/while/body/eval_jaxpr/nsi,sr->nri/dot_general | solution.py:34
  296.5 10.4 %bitcast_add_fusion.5 = f32[256,64,128]{2,1,0:T(8,128)} fusion(f32[256,64,128]{2,1,0:T(8,128)} %get-tuple-element.1006, f32[64,256,128]{2,0,1:T(8,128)} %fusion.97, pred[]{:T(512)S(6)} %compare.7, bf16[256,10,128]{2,1,0:T(8,128)(2,1)S(1)} %copy.86, s32[10]{0:T(128)S(1)} %get-tuple-element.987), kind=kOutput, calls=%fused_computation.16.clone.1 | convolution fusion | flops 48235136 | bytes 25821224 | tf_op jit(solution)/shard_map/while/body/eval_jaxpr/while/body/eval_jaxpr/nsi,sr->nri/dot_general | solution.py:34
  317.0 10.4 %bitcast_add_fusion.5 = f32[256,64,128]{2,1,0:T(8,128)} fusion(f32[256,64,128]{2,1,0:T(8,128)} %get-tuple-element.1006, f32[64,256,128]{2,0,1:T(8,128)} %fusion.97, pred[]{:T(512)S(6)} %compare.7, bf16[256,10,128]{2,1,0:T(8,128)(2,1)S(1)} %copy.86, s32[10]{0:T(128)S(1)} %get-tuple-element.987), kind=kOutput, calls=%fused_computation.16.clone.1 | convolution fusion | flops 48235136 | bytes 25821224 | tf_op jit(solution)/shard_map/while/body/eval_jaxpr/while/body/eval_jaxpr/nsi,sr->nri/dot_general | solution.py:34
  337.5 10.4 %bitcast_add_fusion.5 = f32[256,64,128]{2,1,0:T(8,128)} fusion(f32[256,64,128]{2,1,0:T(8,128)} %get-tuple-element.1006, f32[64,256,128]{2,0,1:T(8,128)} %fusion.97, pred[]{:T(512)S(6)} %compare.7, bf16[256,10,128]{2,1,0:T(8,128)(2,1)S(1)} %copy.86, s32[10]{0:T(128)S(1)} %get-tuple-element.987), kind=kOutput, calls=%fused_computation.16.clone.1 | convolution fusion | flops 48235136 | bytes 25821224 | tf_op jit(solution)/shard_map/while/body/eval_jaxpr/while/body/eval_jaxpr/nsi,sr->nri/dot_general | solution.py:34
  358.1 10.4 %bitcast_add_fusion.5 = f32[256,64,128]{2,1,0:T(8,128)} fusion(f32[256,64,128]{2,1,0:T(8,128)} %get-tuple-element.1006, f32[64,256,128]{2,0,1:T(8,128)} %fusion.97, pred[]{:T(512)S(6)} %compare.7, bf16[256,10,128]{2,1,0:T(8,128)(2,1)S(1)} %copy.86, s32[10]{0:T(128)S(1)} %get-tuple-element.987), kind=kOutput, calls=%fused_computation.16.clone.1 | convolution fusion | flops 48235136 | bytes 25821224 | tf_op jit(solution)/shard_map/while/body/eval_jaxpr/while/body/eval_jaxpr/nsi,sr->nri/dot_general | solution.py:34
  388.1 47.2 %while.104 = (s32[]{:T(128)}, f32[80,128,128]{2,1,0:T(8,128)}, s32[80]{0:T(128)S(1)}, bf16[256,64,128]{2,1,0:T(8,128)(2,1)}, bf16[256,20,128]{2,1,0:T(8,128)(2,1...) while((s32[]{:T(128)}, f32[80,128,128]{2,1,0:T(8,128)}, s32[80]{0:T(128)S(1)}, ...), condition=%wide.region_7.7_spmd, body=%wide.region_6.6_spmd.sunk | while | flops 139756480 | bytes 9437531 | solution.py:48
  437.8 161.9 %while.103 = (s32[]{:T(128)}, f32[256,64,128]{2,1,0:T(8,128)}, s32[80]{0:T(128)S(1)}, bf16[80,128,128]{2,1,0:T(8,128)(2,1)}, bf16[256,20,128]{2,1,0:T(8,128)(2,1...) while((s32[]{:T(128)}, f32[256,64,128]{2,1,0:T(8,128)}, s32[80]{0:T(128)S(1)}, ...), condition=%wide.region_5.5_spmd.clone, body=%wide.region_4.4_spmd.clone.sunk | while | flops 188810816 | bytes 41746828 | solution.py:48
  466.2 10.4 %bitcast_add_fusion.5 = f32[256,64,128]{2,1,0:T(8,128)} fusion(f32[256,64,128]{2,1,0:T(8,128)} %get-tuple-element.1006, f32[64,256,128]{2,0,1:T(8,128)} %fusion.97, pred[]{:T(512)S(6)} %compare.7, bf16[256,10,128]{2,1,0:T(8,128)(2,1)S(1)} %copy.86, s32[10]{0:T(128)S(1)} %get-tuple-element.987), kind=kOutput, calls=%fused_computation.16.clone.1 | convolution fusion | flops 48235136 | bytes 25821224 | tf_op jit(solution)/shard_map/while/body/eval_jaxpr/while/body/eval_jaxpr/nsi,sr->nri/dot_general | solution.py:34
  486.7 10.4 %bitcast_add_fusion.5 = f32[256,64,128]{2,1,0:T(8,128)} fusion(f32[256,64,128]{2,1,0:T(8,128)} %get-tuple-element.1006, f32[64,256,128]{2,0,1:T(8,128)} %fusion.97, pred[]{:T(512)S(6)} %compare.7, bf16[256,10,128]{2,1,0:T(8,128)(2,1)S(1)} %copy.86, s32[10]{0:T(128)S(1)} %get-tuple-element.987), kind=kOutput, calls=%fused_computation.16.clone.1 | convolution fusion | flops 48235136 | bytes 25821224 | tf_op jit(solution)/shard_map/while/body/eval_jaxpr/while/body/eval_jaxpr/nsi,sr->nri/dot_general | solution.py:34
  507.2 10.4 %bitcast_add_fusion.5 = f32[256,64,128]{2,1,0:T(8,128)} fusion(f32[256,64,128]{2,1,0:T(8,128)} %get-tuple-element.1006, f32[64,256,128]{2,0,1:T(8,128)} %fusion.97, pred[]{:T(512)S(6)} %compare.7, bf16[256,10,128]{2,1,0:T(8,128)(2,1)S(1)} %copy.86, s32[10]{0:T(128)S(1)} %get-tuple-element.987), kind=kOutput, calls=%fused_computation.16.clone.1 | convolution fusion | flops 48235136 | bytes 25821224 | tf_op jit(solution)/shard_map/while/body/eval_jaxpr/while/body/eval_jaxpr/nsi,sr->nri/dot_general | solution.py:34
  527.7 10.4 %bitcast_add_fusion.5 = f32[256,64,128]{2,1,0:T(8,128)} fusion(f32[256,64,128]{2,1,0:T(8,128)} %get-tuple-element.1006, f32[64,256,128]{2,0,1:T(8,128)} %fusion.97, pred[]{:T(512)S(6)} %compare.7, bf16[256,10,128]{2,1,0:T(8,128)(2,1)S(1)} %copy.86, s32[10]{0:T(128)S(1)} %get-tuple-element.987), kind=kOutput, calls=%fused_computation.16.clone.1 | convolution fusion | flops 48235136 | bytes 25821224 | tf_op jit(solution)/shard_map/while/body/eval_jaxpr/while/body/eval_jaxpr/nsi,sr->nri/dot_general | solution.py:34
  548.3 10.4 %bitcast_add_fusion.5 = f32[256,64,128]{2,1,0:T(8,128)} fusion(f32[256,64,128]{2,1,0:T(8,128)} %get-tuple-element.1006, f32[64,256,128]{2,0,1:T(8,128)} %fusion.97, pred[]{:T(512)S(6)} %compare.7, bf16[256,10,128]{2,1,0:T(8,128)(2,1)S(1)} %copy.86, s32[10]{0:T(128)S(1)} %get-tuple-element.987), kind=kOutput, calls=%fused_computation.16.clone.1 | convolution fusion | flops 48235136 | bytes 25821224 | tf_op jit(solution)/shard_map/while/body/eval_jaxpr/while/body/eval_jaxpr/nsi,sr->nri/dot_general | solution.py:34
  568.8 10.4 %bitcast_add_fusion.5 = f32[256,64,128]{2,1,0:T(8,128)} fusion(f32[256,64,128]{2,1,0:T(8,128)} %get-tuple-element.1006, f32[64,256,128]{2,0,1:T(8,128)} %fusion.97, pred[]{:T(512)S(6)} %compare.7, bf16[256,10,128]{2,1,0:T(8,128)(2,1)S(1)} %copy.86, s32[10]{0:T(128)S(1)} %get-tuple-element.987), kind=kOutput, calls=%fused_computation.16.clone.1 | convolution fusion | flops 48235136 | bytes 25821224 | tf_op jit(solution)/shard_map/while/body/eval_jaxpr/while/body/eval_jaxpr/nsi,sr->nri/dot_general | solution.py:34
  589.3 10.4 %bitcast_add_fusion.5 = f32[256,64,128]{2,1,0:T(8,128)} fusion(f32[256,64,128]{2,1,0:T(8,128)} %get-tuple-element.1006, f32[64,256,128]{2,0,1:T(8,128)} %fusion.97, pred[]{:T(512)S(6)} %compare.7, bf16[256,10,128]{2,1,0:T(8,128)(2,1)S(1)} %copy.86, s32[10]{0:T(128)S(1)} %get-tuple-element.987), kind=kOutput, calls=%fused_computation.16.clone.1 | convolution fusion | flops 48235136 | bytes 25821224 | tf_op jit(solution)/shard_map/while/body/eval_jaxpr/while/body/eval_jaxpr/nsi,sr->nri/dot_general | solution.py:34
  604.2 10.1 %bitcast_dynamic-update-slice_fusion.3 = bf16[512,8192]{1,0:T(8,128)(2,1)} fusion(bf16[512,8192]{1,0:T(8,128)(2,1)} %get-tuple-element.1097, s32[]{:T(128)S(6)} %select_n.148, bf16[32,8,64,128]{3,2,1,0:T(8,128)(2,1)S(1)} %bitcast.116), kind=kLoop, calls=%fused_computation.34.clone.1 | loop fusion | bytes 8388612 | tf_op jit(solution)/shard_map/while/body/eval_jaxpr/dynamic_update_slice | solution.py:115
  619.4 47.2 %while.104 = (s32[]{:T(128)}, f32[80,128,128]{2,1,0:T(8,128)}, s32[80]{0:T(128)S(1)}, bf16[256,64,128]{2,1,0:T(8,128)(2,1)}, bf16[256,20,128]{2,1,0:T(8,128)(2,1...) while((s32[]{:T(128)}, f32[80,128,128]{2,1,0:T(8,128)}, s32[80]{0:T(128)S(1)}, ...), condition=%wide.region_7.7_spmd, body=%wide.region_6.6_spmd.sunk | while | flops 139756480 | bytes 9437531 | solution.py:48
  671.8 198.4 %while.102 = (s32[]{:T(128)}, f32[512,20,128]{2,1,0:T(8,128)}, s32[80]{0:T(128)S(1)}, bf16[80,128,128]{2,1,0:T(8,128)(2,1)}, bf16[512,64,128]{2,1,0:T(8,128)(2,1...) while((s32[]{:T(128)}, f32[512,20,128]{2,1,0:T(8,128)}, s32[80]{0:T(128)S(1)}, ...), condition=%wide.region_2.3_spmd.clone, body=%wide.region_1.2_spmd.clone.sunk | while | flops 311297152 | bytes 42795404 | solution.py:48
  889.7 49.9 %all-gather.10.cloned.1.call-done = f32[262144]{0:T(1024)} async-done(((f32[8192]{0:T(1024)}), f32[262144]{0:T(1024)}) %all-gather.10.cloned.1.call-update) | async-done | bytes 1048592 | tf_op jit(solution)/shard_map/all_gather | solution.py:130
  (281 shorter events, 568.2 us)
Async XLA Ops:
  7.2 7.1 copy-start.2
  7.2 8.0 copy-start.1
  7.2 158.8 %all-gather.8.cloned.1.call-start = ((), (), s32[]{:S(2)}) async-start(), calls=%async_computation.3 | async-start | bytes 10485760 | tf_op jit(solution)/shard_map/all_gather | solution.py:62
  9.5 0.5 copy-start.4
  13.5 4.3 copy-start.7
  13.5 5.5 copy-start.6
  13.5 183.3 %all-gather.6.cloned.1.call-start = ((), (), s32[]{:S(2)}) async-start(), calls=%async_computation.2 | async-start | bytes 2949120 | tf_op jit(solution)/shard_map/all_gather | solution.py:73
  15.1 864.9 %reduce-scatter.5.cloned.1.call-start = ((), (), s32[]{:S(2)}) async-start(), calls=%async_computation.5 | async-start | bytes 2949120 | tf_op jit(solution)/shard_map/reduce_scatter | solution.py:124
  671.2 210.8 %reduce-scatter.3.cloned.1.call-start = ((), (), s32[]{:S(2)}) async-start(), calls=%async_computation.4 | async-start | bytes 10485760 | tf_op jit(solution)/shard_map/reduce_scatter | solution.py:121
  671.7 267.8 %all-gather.10.cloned.1.call-start = ((), (), s32[]{:S(2)}) async-start(), calls=%async_computation.6 | async-start | bytes 1081344 | tf_op jit(solution)/shard_map/all_gather | solution.py:130
  875.5 6.5 copy-start
  875.5 6.5 copy-start.3
  875.5 6.5 copy-start.5
Sparse Core Ops, SparseCore 0:
  13.7 152.3 all-gather.7
  168.5 28.3 all-gather.5
  671.3 43.6 reduce-scatter.4
  717.2 144.4 reduce-scatter.2
  885.8 53.6 all-gather.9
